TPU v7x, 128 devices: a whole 4x4x4 slice. The times are simulated.
128 devices in a mesh: grp: 4 (over y), cur: 32 (over x, z, core).
Axes of the slice: x: 4, y: 4, z: 4, core: 2. Of those that a mesh axis runs over, the one named last changes fastest.
Arguments:
- fine_state: bfloat16 [786432, 256], P(('grp', 'cur')), may hold values from -8 to 8
- send_index: int32 [128, 2, 256], P(('grp', 'cur')), may hold values from 0 to 6143
- edge_src: int32 [128, 36864], P(('grp', 'cur')), may hold values from 0 to 6655, as said below
- edge_dst: int32 [128, 36864], P(('grp', 'cur')), may hold values from 0 to 6144, as said below
- cell_slot: int32 [786432], P(('grp', 'cur')), may hold values from 0 to 96, as said below
- slot_parent: int32 [128, 97], P(('grp', 'cur')), may hold values from 0 to 3071, as said below
- w_src: bfloat16 [256, 256], replicated, may hold values from -0.375 to 0.375
- w_dst: bfloat16 [256, 256], replicated, may hold values from -0.375 to 0.375
- msg_bias: float32 [256], replicated, may hold values from -4 to 4
- w_msg: bfloat16 [256, 256], replicated, may hold values from -0.375 to 0.375
- w_upd: bfloat16 [256, 256], replicated, may hold values from -0.375 to 0.375
- w_pool: bfloat16 [256, 1024], replicated, may hold values from -3 to 3
- norm_gain: float32 [1024], replicated, may hold values from 0.1 to 1.9
- w_query: bfloat16 [1024, 1024], replicated, may hold values from -1 to 1
- w_key: bfloat16 [1024, 256], replicated, may hold values from -1 to 1
- w_value: bfloat16 [1024, 256], replicated, may hold values from -0.1875 to 0.1875
- w_out: bfloat16 [1024, 1024], replicated, may hold values from -0.1875 to 0.1875
- head_scale: float32 [8], replicated, may hold values from 2 to 16
Outputs:
- fine_out: bfloat16 [786432, 256], P(('grp', 'cur'))
- coarse_out: bfloat16 [12288, 1024], P(('grp', 'cur'))
Inputs may be any that keep to these rules, and one draw needn't show every extreme that they name: `edge_src`: slots from a device's live count on hold 0; live slots name any entry of the device's table. `edge_dst`: the value 6144 marks a padded slot. On each device the live slots come first and number between half of 36864 and all of it; some device has all slots live. `cell_slot`: cells of one device that share a slot are consecutive and have one parent; every slot 0 to 96 is used on every device. `slot_parent`: A parent numbered p within its group is owned by the device of that group with cur index p // 96, at row p % 96. Each of a group's parents has exactly 64 cells, all on one device or on two consecutive devices of the group. On each device at most 4 slots name parents of one owner, and some owner receives exactly 4 from every device of its group.
All inputs are finite; a program needn't handle non-finite values.
Results may differ from a plain program's by a relative error of at most 0.005.
Values may be sent and summed in bfloat16 or wider, within the bound.
No kernel may reach another device: no remote copies, remote signals or barrier semaphores. Data moves between devices by JAX's collectives and lax.ppermute only.
A program may use at most 128 MiB of HBM per device.

v0:
```python
import functools
import math
import jax, jax.numpy as jnp
from jax import lax
from jax.experimental import pallas as pl
from jax.experimental.pallas import tpu as pltpu
from jax.sharding import PartitionSpec as P

TILE = 256
WINDOW = 128
TOGETHER = 4
TARGET_SHIFT = 13
NO_TARGET = 6144
SLOT_ROWS = 104
SLOTS = 97
bf16, f32, i32 = jnp.bfloat16, jnp.float32, jnp.int32


def sort_kernel(source_ref, target_ref, rows_ref, targets_ref, key):
    given = source_ref.shape[0]
    fill = jnp.full((8, 128), NO_TARGET << TARGET_SHIFT, i32)
    held = [(target_ref[v] << TARGET_SHIFT) | source_ref[v] if v < given else fill for v in range(64)]
    for phase in range(1, 6):
        for bit in range(phase - 1, -1, -1):
            for v in range(64):
                if not v >> bit & 1:
                    w = v | 1 << bit
                    small, large = jnp.minimum(held[v], held[w]), jnp.maximum(held[v], held[w])
                    held[v], held[w] = (large, small) if v >> phase & 1 else (small, large)
    for v in range(64):
        key[v >> 3, v & 7] = held[v]
    row = lax.broadcasted_iota(i32, (8, 128), 0)
    lane = lax.broadcasted_iota(i32, (8, 128), 1)

    def bit_of(bit):
        if bit == 16:
            return jnp.zeros((8, 128), i32)
        return (row >> (bit - 6) & 1) if bit < 9 else (lane >> (bit - 9) & 1)

    for phase in range(6, 17):
        flip = bit_of(phase) if phase == 6 else bit_of(phase) ^ bit_of(phase - 1)

        def across(g, carry):
            held = key[pl.ds(2 * g, 2)].reshape(16, 8, 128) ^ (-flip)[None]
            for bit in range(phase - 1, 5, -1):
                axis, by, size = (1, 1 << (bit - 6), 8) if bit < 9 else (2, 1 << (bit - 9), 128)
                upper = (bit_of(bit) == 1)[None]
                if 2 * by == size:
                    other = pltpu.roll(held, by, axis)
                else:
                    other = jnp.where(upper, pltpu.roll(held, by, axis), pltpu.roll(held, size - by, axis))
                held = jnp.where(upper, jnp.maximum(held, other), jnp.minimum(held, other))
            key[pl.ds(2 * g, 2)] = held.reshape(2, 8, 8, 128)
            return carry

        lax.fori_loop(0, 4, across, 0, unroll=4)

        def merge(held):
            for bit in (2, 1, 0):
                pairs = held.reshape(4 >> bit, 2, 1 << bit, 8, 128)
                held = jnp.stack(
                    [jnp.minimum(pairs[:, 0], pairs[:, 1]), jnp.maximum(pairs[:, 0], pairs[:, 1])], axis=1
                ).reshape(8, 8, 128)
            return held

        def high(g, carry):
            key[:, g] = merge(key[:, g])
            return carry

        def low(g, carry):
            key[g] = merge(key[g])
            return carry

        lax.fori_loop(0, 8, high, 0, unroll=8)
        lax.fori_loop(0, 8, low, 0, unroll=8)

    flat = key.reshape(512, 128)
    half = rows_ref.shape[1] // 2
    for part in range(4):
        piece = jnp.concatenate([flat[pl.ds(s, 64, stride=8), :] for s in (2 * part, 2 * part + 1)], axis=0)
        piece = jnp.transpose(piece)[:half]
        at = (part % 2, pl.ds(part // 2, half, stride=2), slice(None))
        rows_ref[at] = (piece & ((1 << TARGET_SHIFT) - 1)) * 2
        targets_ref[at] = piece >> TARGET_SHIFT


def sorted_edges(source, target):
    edges = source.shape[0]
    shape = jax.ShapeDtypeStruct((2, edges // TILE, 128), i32)
    return pl.pallas_call(
        sort_kernel,
        out_shape=(shape, shape),
        scratch_shapes=[pltpu.VMEM((8, 8, 8, 128), i32)],
        compiler_params=pltpu.CompilerParams(vmem_limit_bytes=24 << 20),
        name="sort_edges",
    )(source.reshape(-1, 8, 128), target.reshape(-1, 8, 128))


def fine_kernel(rows_ref, start_ref, windows_ref, pairs_ref, local_ref, slot_ref, parent_ref, own_ref, before_ref, after_ref, w_src_ref, w_dst_ref,
                bias_ref, w_msg_ref, w_upd_ref, out_ref, part_ref, table, dst, total, count, got_a, got_b):
    blocks = own_ref.shape[0] // TILE
    tiles_most = local_ref.shape[1]

    def put_table(places, groups):
        projs = [jnp.dot(rows, w_src_ref[...], preferred_element_type=f32).astype(bf16).astype(f32) for rows in groups]
        for place, proj in zip(places, projs):
            proj = proj + bias_ref[...]
            table[pl.ds(2 * place, TILE, stride=2), :] = proj[:, :128]
            table[pl.ds(2 * place + 1, TILE, stride=2), :] = proj[:, 128:]

    def project(j, carry):
        places = [pl.multiple_of((j * TOGETHER + n) * TILE, TILE) for n in range(TOGETHER)]
        groups = [own_ref[pl.ds(at, TILE), :] for at in places]
        put_table(places, groups)
        mine = [jnp.dot(own, w_dst_ref[...], preferred_element_type=f32).astype(bf16) for own in groups]
        for at, proj in zip(places, mine):
            dst[pl.ds(at, TILE), :] = proj
            total[pl.ds(at, TILE), :] = jnp.zeros((TILE, 256), f32)
            count[pl.ds(at, TILE), :] = jnp.zeros((TILE, 128), f32)
        return carry

    lax.fori_loop(0, blocks // TOGETHER, project, 0)
    put_table((blocks * TILE, blocks * TILE + TILE), (before_ref[...], after_ref[...]))

    place = lax.broadcasted_iota(i32, (WINDOW, TILE), 0).astype(f32).astype(bf16)
    one, zero = jnp.ones((WINDOW, TILE), bf16), jnp.zeros((WINDOW, TILE), bf16)
    ones = jnp.ones((TILE, 128), bf16)

    def fetch(base, first, last, got):
        for i in range(first, last):
            place = i % TILE // 128 * (tiles_most * 128) + i // TILE * 128 + i % 128
            got[2 * i:2 * i + 2, :] = table[pl.ds(rows_ref[base + place], 2), :]

    def tile_steps(tile, n, got, start):
        state = {}

        def first():
            state["at"] = at = pl.multiple_of(start, 16)
            local = jnp.concatenate([local_ref[k, pl.ds(tile, 1), :] for k in range(2)], axis=1)
            local = jnp.minimum(local - at, WINDOW).astype(f32).astype(bf16)
            state["hot"] = jnp.where(place == local, one, zero)
            state["own"] = lax.dot_general(
                state["hot"], dst[pl.ds(at, WINDOW), :], (((0,), (0,)), ((), ())), preferred_element_type=f32
            )

        def second():
            sent = [got[pl.ds(2 * TILE * n + k, TILE, stride=2), :] for k in range(2)]
            half = 0.5 * (state["own"] + jnp.concatenate(sent, axis=1))
            state["hidden"] = (half + half * jnp.tanh(half)).astype(bf16)

        def third():
            at = pl.ds(state["at"], WINDOW)
            total[at, :] += jnp.dot(state["hot"], state["hidden"], preferred_element_type=f32)
            count[at, :] += jnp.dot(state["hot"], ones, preferred_element_type=f32)

        return first, second, third

    def advance(tile, got, ahead, got_ahead):
        base = jnp.minimum(ahead, tiles_most - TOGETHER) * 128
        tiles = [tile_steps(tile + n, n, got, start_ref[tile + n]) for n in range(TOGETHER)]
        steps = [run for steps in zip(*tiles) for run in steps]
        rows = TOGETHER * TILE
        for i, run in enumerate(steps):
            fetch(base, rows * i // len(steps), rows * (i + 1) // len(steps), got_ahead)
            run()

    def step(j, carry):
        tile = 2 * TOGETHER * j
        advance(tile, got_a, tile + TOGETHER, got_b)
        advance(tile + TOGETHER, got_b, tile + 2 * TOGETHER, got_a)
        return carry

    fetch(0, 0, TOGETHER * TILE, got_a)
    lax.fori_loop(0, pairs_ref[0], step, 0)

    def rest(tile, carry):
        def window(w, carry):
            fetch(tile * 128, 0, TILE, got_a)
            for run in tile_steps(tile, 0, got_a, jnp.minimum(start_ref[tile] + w * WINDOW, blocks * TILE - WINDOW)):
                run()
            return carry

        return lax.fori_loop(1, windows_ref[tile], window, carry)

    lax.fori_loop(0, tiles_most, rest, 0)

    slots = lax.broadcasted_iota(i32, (SLOT_ROWS, TILE), 0)

    row = lax.broadcasted_iota(i32, (SLOT_ROWS, 256), 0)
    high = jnp.where(row == SLOTS, parent_ref[...] >> 6, 0)
    tags = jnp.where(row == SLOTS + 1, parent_ref[...] & 63, high).astype(f32)

    def finish(j, parts):
        group = [j * TOGETHER + n for n in range(TOGETHER)]
        spots = [pl.ds(pl.multiple_of(b * TILE, TILE), TILE) for b in group]
        w_msg = w_msg_ref[...]
        highs, lows = [], []
        for at in spots:
            scale = 1.0 / jnp.maximum(count[at, :], 1.0)
            mean = total[at, :] * jnp.concatenate([scale, scale], axis=1)
            highs.append(mean.astype(bf16))
            lows.append((mean - highs[-1].astype(f32)).astype(bf16))
        aggs = [
            jnp.dot(high, w_msg, preferred_element_type=f32) + jnp.dot(low, w_msg, preferred_element_type=f32)
            for high, low in zip(highs, lows)
        ]
        updates = [jnp.dot(agg.astype(bf16), w_upd_ref[...], preferred_element_type=f32) for agg in aggs]
        for b, at, update in zip(group, spots, updates):
            new = (own_ref[at, :].astype(f32) + update).astype(bf16)
            out_ref[at, :] = new
            hot = (slots == slot_ref[b]).astype(f32).astype(bf16)
            parts += jnp.dot(hot, new, preferred_element_type=f32)
        return parts

    parts = lax.fori_loop(0, blocks // TOGETHER, finish, tags)
    part_ref[...] = parts.astype(bf16)


def fine_pass(own, before, after, source, target, cell_slot, parents, w_src, w_dst, bias, w_msg, w_upd):
    cells = own.shape[0]
    blocks = cells // TILE
    tiles = source.shape[0] // TILE
    rows, targets = sorted_edges(source, target)
    start = jnp.minimum(targets[0, :, 0] & -16, cells - WINDOW)
    last = jnp.max(jnp.where(targets < cells, targets, -1), axis=(0, 2))
    windows = jnp.maximum(last + WINDOW - start, 0) // WINDOW
    pairs = (jnp.sum((last >= 0).astype(i32)) + (2 * TOGETHER - 1)) // (2 * TOGETHER)
    smem = pl.BlockSpec(memory_space=pltpu.SMEM)
    vmem = pl.BlockSpec(memory_space=pltpu.VMEM)
    return pl.pallas_call(
        fine_kernel,
        out_shape=(jax.ShapeDtypeStruct(own.shape, bf16), jax.ShapeDtypeStruct((SLOT_ROWS, 256), bf16)),
        in_specs=[smem] * 4 + [vmem] * 11,
        out_specs=(vmem, vmem),
        scratch_shapes=[
            pltpu.VMEM((2 * (cells + 2 * TILE), 128), f32),
            pltpu.VMEM((cells, 256), bf16),
            pltpu.VMEM((cells, 256), f32),
            pltpu.VMEM((cells, 128), f32),
            pltpu.VMEM((2 * TOGETHER * TILE, 128), f32),
            pltpu.VMEM((2 * TOGETHER * TILE, 128), f32),
        ],
        compiler_params=pltpu.CompilerParams(vmem_limit_bytes=58 << 20),
        name="fine_cells",
    )(rows.reshape(-1), start, windows, pairs[None], targets, cell_slot.reshape(blocks, 1, TILE), parents, own, before, after, w_src, w_dst,
      bias.reshape(1, -1), w_msg, w_upd)


def moved(value, axis, pairs):
    return lax.ppermute(value, axis, pairs)


def ring_gather(value, move):
    return jnp.concatenate([value] + [move(value, by) for by in (1, 3, 2)], axis=0)


def gather_group(part):
    devices = lax.axis_size("cur")

    def along_z(value, by):
        return lax.ppermute(value, "cur", [(i, i // 8 * 8 + (i + 2 * by) % 8) for i in range(devices)])

    def along_x(value, by):
        return lax.ppermute(value, "cur", [(i, (i + 8 * by) % devices) for i in range(devices)])

    rows = ring_gather(part[None], along_z)
    rows = ring_gather(rows, along_x)
    return jnp.concatenate([rows, lax.ppermute(rows, "cur", [(i, i ^ 1) for i in range(devices)])], axis=0)


def normed_parents(firsts, label_ref, rows_ref, w_pool_ref, gain_ref, parents):
    shape = (parents, rows_ref.shape[0])
    ids = lax.broadcasted_iota(i32, shape, 0).astype(f32).astype(bf16)
    one, zero = jnp.ones(shape, bf16), jnp.zeros(shape, bf16)
    labels = [jnp.clip(label_ref[...] - first, -1, 256).astype(f32).astype(bf16) for first in firsts]
    sums = [jnp.dot(jnp.where(ids == label, one, zero), rows_ref[...], preferred_element_type=f32) for label in labels]
    means = [(total * (1.0 / 64.0)).astype(bf16) for total in sums]
    coarse = [jnp.dot(mean, w_pool_ref[...], preferred_element_type=f32) for mean in means]
    inverse = [lax.rsqrt(jnp.mean(rows * rows, axis=1, keepdims=True) + 1e-06) for rows in coarse]
    return coarse, [(rows * scale * gain_ref[...]).astype(bf16) for rows, scale in zip(coarse, inverse)]


def query_kernel(first_ref, label_ref, rows_ref, w_pool_ref, gain_ref, w_query_ref, coarse_ref, query_ref):
    coarse, normed = normed_parents([first_ref[0]], label_ref, rows_ref, w_pool_ref, gain_ref, query_ref.shape[0])
    coarse_ref[...] = coarse[0]
    query_ref[...] = jnp.dot(normed[0], w_query_ref[...], preferred_element_type=f32).astype(bf16)


def key_kernel(label_ref, rows_ref, w_pool_ref, gain_ref, w_key_ref, w_value_ref, key_ref, value_ref):
    most = 256
    parts = value_ref.shape[0] // most
    firsts = [pl.program_id(0) * value_ref.shape[0] + part * most for part in range(parts)]
    normed = normed_parents(firsts, label_ref, rows_ref, w_pool_ref, gain_ref, most)[1]
    keys = [jnp.dot(rows, w_key_ref[...], preferred_element_type=f32) for rows in normed]
    values = [jnp.dot(rows, w_value_ref[...], preferred_element_type=f32) for rows in normed]
    for part in range(parts):
        at = slice(part * most, (part + 1) * most)
        value_ref[at, :] = values[part].astype(bf16)
        key_ref[:, at] = jnp.transpose(keys[part]).astype(bf16)


def halo_kernel(index_ref, own_ref, before_ref, after_ref):
    lane = lax.broadcasted_iota(i32, (128, 128), 1)
    wanted = [jnp.transpose(jnp.broadcast_to(index_ref[r:r + 1, :], (128, 128))) - lane for r in range(4)]
    step = 1024
    found = 0.0
    for start in range(0, own_ref.shape[0], step):
        hot = jnp.concatenate(
            [jnp.concatenate([(w == start + t).astype(f32).astype(bf16) for t in range(0, step, 128)], axis=1) for w in wanted],
            axis=0,
        )
        found += jnp.dot(hot, own_ref[start:start + step, :], preferred_element_type=f32)
    half = before_ref.shape[0]
    before_ref[...] = found[:half].astype(bf16)
    after_ref[...] = found[half:].astype(bf16)


def attend_kernel(factor_ref, key_ref, value_ref, *refs):
    query_refs, out_refs = refs[:len(refs) // 2], refs[len(refs) // 2:]
    rows = query_refs[0].shape[0]
    chunk = value_ref.shape[0] // 4
    chunks = [slice(c, c + chunk) for c in range(0, value_ref.shape[0], chunk)]
    ones = jnp.ones((chunk, 128), bf16)
    scores = []
    for g in range(2):
        scaled = jnp.concatenate(
            [ref[:, h * 128:(h + 1) * 128].astype(f32) * factor_ref[h] for ref in query_refs for h in range(4 * g, 4 * g + 4)],
            axis=0,
        )
        high = scaled.astype(bf16)
        low = (scaled - high.astype(f32)).astype(bf16)
        query = jnp.concatenate([high, low], axis=1)
        own = slice(g * 128, (g + 1) * 128)
        scores.append(
            [jnp.dot(query, jnp.concatenate([key_ref[own, c]] * 2, axis=0), preferred_element_type=f32) for c in chunks]
        )
    levels = [jnp.zeros((rows, 128), f32) for ref in out_refs]
    lanes = lax.broadcasted_iota(i32, (rows, 128), 1)
    for g in range(2):
        own = slice(g * 128, (g + 1) * 128)
        top = functools.reduce(jnp.maximum, [jnp.max(score, axis=1, keepdims=True) for score in scores[g]])
        both = 0.0
        for score, c in zip(scores[g], chunks):
            weight = jnp.exp2(score - top).astype(bf16)
            both += jnp.dot(weight, jnp.concatenate([value_ref[c, own], ones], axis=1), preferred_element_type=f32)
        norm = both[:, 128:]
        attn = (both[:, :128] / norm).astype(bf16)
        level = top + jnp.log2(norm)
        for n, out_ref in enumerate(out_refs):
            for r in range(4):
                h = 4 * g + r
                at = slice((4 * n + r) * rows, (4 * n + r + 1) * rows)
                out_ref[:, h * 128:(h + 1) * 128] = attn[at]
                levels[n] = jnp.where(lanes == h, level[at], levels[n])
    for level, out_ref in zip(levels, out_refs):
        high = level.astype(bf16)
        rest = level - high.astype(f32)
        middle = rest.astype(bf16)
        out_ref[:, 1024:1152] = high
        out_ref[:, 1152:1280] = middle
        out_ref[:, 1280:1408] = (rest - middle.astype(f32)).astype(bf16)


def merge_kernel(a_ref, b_ref, c_ref, d_ref, coarse_ref, w_out_ref, out_ref):
    refs = (a_ref, b_ref, c_ref, d_ref)
    levels = [r[:, 1024:1152].astype(f32) + (r[:, 1152:1280].astype(f32) + r[:, 1280:1408].astype(f32)) for r in refs]
    top = jnp.maximum(jnp.maximum(levels[0], levels[1]), jnp.maximum(levels[2], levels[3]))
    shares = [jnp.exp2(level - top) for level in levels]
    whole = shares[0] + shares[1] + shares[2] + shares[3]
    shares = [share / whole for share in shares]
    pieces = []
    for h in range(8):
        at = slice(h * 128, (h + 1) * 128)
        pieces.append(sum(r[:, at].astype(f32) * s[:, h:h + 1] for r, s in zip(refs, shares)))
    attn = jnp.concatenate(pieces, axis=1).astype(bf16)
    out_ref[...] = (coarse_ref[...] + jnp.dot(attn, w_out_ref[...], preferred_element_type=f32)).astype(bf16)


def body(fine_state, send_index, edge_src, edge_dst, cell_slot, slot_parent, w_src, w_dst, msg_bias, w_msg, w_upd,
         w_pool, norm_gain, w_query, w_key, w_value, w_out, head_scale):
    groups, devices = lax.axis_size("grp"), lax.axis_size("cur")
    smem = pl.BlockSpec(memory_space=pltpu.SMEM)
    vmem = pl.BlockSpec(memory_space=pltpu.VMEM)
    every = groups * devices
    both = ("grp", "cur")
    limit = lambda size: pltpu.CompilerParams(vmem_limit_bytes=size << 20)
    halo = send_index.shape[2]
    to_next, to_prev = pl.pallas_call(
        halo_kernel,
        out_shape=[jax.ShapeDtypeStruct((halo, fine_state.shape[1]), bf16)] * 2,
        in_specs=[vmem] * 2,
        out_specs=[vmem] * 2,
        compiler_params=limit(16),
        name="halo_cells",
    )(send_index.reshape(-1, 128), fine_state)
    before = lax.ppermute(to_next, both, [(i, (i + 1) % every) for i in range(every)])
    after = lax.ppermute(to_prev, both, [(i, (i - 1) % every) for i in range(every)])
    slots = slot_parent.shape[1]
    par_dev = slots - 1
    parents = jnp.pad(slot_parent, ((0, 0), (0, 256 - slots)), constant_values=-64)
    fine_out, part = fine_pass(fine_state, before, after, edge_src[0], edge_dst[0], cell_slot, parents,
                               w_src, w_dst, msg_bias, w_msg, w_upd)
    blocks = gather_group(part)
    labels = (blocks[:, slots, :SLOT_ROWS].astype(i32) * 64 + blocks[:, slots + 1, :SLOT_ROWS].astype(i32)).reshape(1, -1)
    rows = blocks.reshape(-1, 256)
    gain = norm_gain.reshape(1, -1)
    width = w_query.shape[1]
    coarse, query = pl.pallas_call(
        query_kernel,
        out_shape=(jax.ShapeDtypeStruct((par_dev, width), f32), jax.ShapeDtypeStruct((par_dev, width), bf16)),
        in_specs=[smem] + [vmem] * 5,
        out_specs=(vmem, vmem),
        compiler_params=limit(16),
        name="own_query",
    )((lax.axis_index("cur") * par_dev)[None], labels, rows, w_pool, gain, w_query)
    query, rows = lax.optimization_barrier((query, rows))
    asked = {by: lax.ppermute(query, "grp", [(i, (i + by) % groups) for i in range(groups)]) for by in (2, 1, 3)}
    asked[0] = query
    known = par_dev * devices
    step = 768
    whole = lambda *shape: pl.BlockSpec(shape, lambda i: (0,) * len(shape))
    keys, values = pl.pallas_call(
        key_kernel,
        out_shape=(jax.ShapeDtypeStruct((256, known), bf16), jax.ShapeDtypeStruct((known, 256), bf16)),
        grid=(known // step,),
        in_specs=[whole(*labels.shape), whole(*rows.shape), whole(*w_pool.shape), whole(*gain.shape),
                  whole(*w_key.shape), whole(*w_value.shape)],
        out_specs=(pl.BlockSpec((256, step), lambda i: (0, i)), pl.BlockSpec((step, 256), lambda i: (i, 0))),
        compiler_params=limit(32),
        name="group_keys",
    )(labels, rows, w_pool, gain, w_key, w_value)
    factor = head_scale * (math.log2(math.e) / math.sqrt(128.0))
    found = []
    for shifts in ((2,), (1, 3), (0,)):
        pieces = pl.pallas_call(
            attend_kernel,
            out_shape=[jax.ShapeDtypeStruct((par_dev, width + 384), bf16) for by in shifts],
            in_specs=[smem] + [vmem] * (2 + len(shifts)),
            out_specs=[vmem for by in shifts],
            compiler_params=limit(40),
            name="attend",
        )(factor, keys, values, *[asked[by] for by in shifts])
        for by, piece in zip(shifts, pieces):
            found.append(lax.ppermute(piece, "grp", [(i, (i - by) % groups) for i in range(groups)]) if by else piece)
    coarse_out = pl.pallas_call(
        merge_kernel,
        out_shape=jax.ShapeDtypeStruct((par_dev, width), bf16),
        in_specs=[vmem] * 6,
        out_specs=vmem,
        compiler_params=limit(12),
        name="merge",
    )(*found, coarse, w_out)
    return fine_out, coarse_out


def solution(mesh):
    line = P(("grp", "cur"), None)
    in_specs = (line, P(("grp", "cur"), None, None), line, line, P(("grp", "cur")), line) + (P(),) * 12
    return jax.shard_map(body, mesh=mesh, in_specs=in_specs, out_specs=(line, line), check_vma=False)
```

profile of v0, /device:TPU:0, one launch (start us, length us, event | category | flops | bytes accessed | tf_op | source)
XLA Modules:
  0.0 148.9 jit_solution(15269317713042941057)
XLA Ops:
  0.6 0.7 reshape.60.index_ref
  1.3 1.9 %copy-done = bf16[6144,256]{1,0:T(8,128)(2,1)S(1)} copy-done((bf16[6144,256]{1,0:T(8,128)(2,1)S(1)}, bf16[6144,256]{1,0:T(8,128)(2,1)}, u32[]{:S(2)}) %copy-start) | copy-done | bytes 3145752
  3.2 1.8 %halo_cells.1 = (bf16[256,256]{1,0:T(8,128)(2,1)S(1)}, bf16[256,256]{1,0:T(8,128)(2,1)S(1)}) custom-call(s32[4,128]{1,0:T(4,128)S(1)} %reshape.60.index_ref, bf16[6144,256]{1,0:T(8,128)(2,1)S(1)} %copy-done), custom_call_target="tpu_custom_call" | custom-call | tf_op jit(solution)/shard_map/halo_cells/pallas_call | solution.py:388
  5.1 0.1 collective-permute-start
  5.1 8.3 %collective-permute-start.1 = (bf16[256,256]{1,0:T(8,128)(2,1)S(1)}, bf16[256,256]{1,0:T(8,128)(2,1)S(1)}, u32[]{:S(2)}, u32[]{:S(2)}) collective-permute-start(bf16[256,256]{1,0:T(8,128)(2,1)S(1)} %get-tuple-element.19), channel_id=1, source_target_pairs={{0,127},{1,0},{2,1},{3,2},{4,3},{5,4},{6,5},{7,6},{8,7},{9,8},{10,... | collective-permute-start | bytes 393224 | tf_op jit(solution)/shard_map/ppermute | solution.py:397
  13.4 10.8 %sort_edges.1 = (s32[2,144,128]{2,1,0:T(8,128)S(1)}, s32[2,144,128]{2,1,0:T(8,128)S(1)}) custom-call(s32[36,8,128]{2,1,0:T(8,128)S(1)} %bitcast.14, s32[36,8,128]{2,1,0:T(8,128)S(1)} %bitcast.15), custom_call_target="tpu_custom_call" | custom-call | tf_op jit(solution)/shard_map/sort_edges/pallas_call | solution.py:90
  24.3 0.7 copy-done.9
  24.9 0.1 minimum_reduce_fusion.start_ref
  25.1 0.1 fusion
  25.2 1.2 fusion.4
  27.1 0.6 pad.4.parent_ref
  27.7 0.6 copy-done.11
  28.3 0.1 copy-done.12
  28.4 50.1 %fine_cells.1 = (bf16[6144,256]{1,0:T(8,128)(2,1)}, bf16[104,256]{1,0:T(8,128)(2,1)}) custom-call(s32[36864]{0:T(1024)} %bitcast.16, s32[144]{0:T(256)} %copy-done.13, s32[144]{0:T(256)} %get-tuple-element.45.windows_ref, s32[1]{0:T(128)} %bitcast.3.pairs_ref, s32[2,144,128]{2,1,0:T(8,128)} %copy-done.4, s32[24,1,256]{2,1,0:T(1,128)} %bitcast.23, ...), custom_call_target="tpu_custom_call" | custom-call | tf_op jit(solution)/shard_map/fine_cells/pallas_call | solution.py:230
  78.4 4.6 %collective-permute-start.3 = (bf16[1,104,256]{2,1,0:T(8,128)(2,1)}, bf16[1,104,256]{2,1,0:T(8,128)(2,1)S(1)}, u32[]{:S(2)}, u32[]{:S(2)}) collective-permute-start(bf16[1,104,256]{2,1,0:T(8,128)(2,1)} %bitcast.20), channel_id=1, source_target_pairs={{0,6},{1,7},{2,0},{3,1},{4,2},{5,3},{6,4},{7,5},{8,14},{9,15},{10,... | collective-permute-start | bytes 159752 | tf_op jit(solution)/shard_map/ppermute | solution.py:261
  83.0 1.4 collective-permute-start.4
  84.4 1.5 constant_dynamic-update-slice_fusion.6
  85.9 3.0 %collective-permute-done.4 = bf16[1,104,256]{2,1,0:T(8,128)(2,1)S(1)} collective-permute-done((bf16[1,104,256]{2,1,0:T(8,128)(2,1)}, bf16[1,104,256]{2,1,0:T(8,128)(2,1)S(1)}, u32[]{:S(2)}, u32[]{:S(2)}) %collective-permute-start.4) | collective-permute-done | bytes 53280 | tf_op jit(solution)/shard_map/ppermute | solution.py:261
  88.9 0.8 pad_maximum_fusion
  89.7 1.6 %collective-permute-start.5 = (bf16[4,104,256]{2,1,0:T(8,128)(2,1)S(1)}, bf16[4,104,256]{2,1,0:T(8,128)(2,1)S(1)}, u32[]{:S(2)}, u32[]{:S(2)}) collective-permute-start(bf16[4,104,256]{2,1,0:T(8,128)(2,1)S(1)} %pad_maximum_fusion), channel_id=1, source_target_pairs={{0,8},{1,9},{2,10},{3,11},{4,12},{5,13},{6,14},{7,15},{8,16},{9,17... | collective-permute-start | bytes 638984 | tf_op jit(solution)/shard_map/ppermute | solution.py:264
  91.3 1.7 %collective-permute-start.6 = (bf16[4,104,256]{2,1,0:T(8,128)(2,1)S(1)}, bf16[4,104,256]{2,1,0:T(8,128)(2,1)S(1)}, u32[]{:S(2)}, u32[]{:S(2)}) collective-permute-start(bf16[4,104,256]{2,1,0:T(8,128)(2,1)S(1)} %pad_maximum_fusion), channel_id=1, source_target_pairs={{0,24},{1,25},{2,26},{3,27},{4,28},{5,29},{6,30},{7,31},{8,0},{9,1... | collective-permute-start | bytes 638984 | tf_op jit(solution)/shard_map/ppermute | solution.py:264
  93.0 1.7 %collective-permute-start.7 = (bf16[4,104,256]{2,1,0:T(8,128)(2,1)S(1)}, bf16[4,104,256]{2,1,0:T(8,128)(2,1)S(1)}, u32[]{:S(2)}, u32[]{:S(2)}) collective-permute-start(bf16[4,104,256]{2,1,0:T(8,128)(2,1)S(1)} %pad_maximum_fusion), channel_id=1, source_target_pairs={{0,16},{1,17},{2,18},{3,19},{4,20},{5,21},{6,22},{7,23},{8,24},{9,... | collective-permute-start | bytes 638984 | tf_op jit(solution)/shard_map/ppermute | solution.py:264
  94.7 0.6 constant_dynamic-update-slice_fusion.5
  95.4 0.6 constant_dynamic-update-slice_fusion.4
  96.0 0.6 constant_dynamic-update-slice_fusion.3
  96.6 4.1 %collective-permute-done.5 = bf16[4,104,256]{2,1,0:T(8,128)(2,1)S(1)} collective-permute-done((bf16[4,104,256]{2,1,0:T(8,128)(2,1)S(1)}, bf16[4,104,256]{2,1,0:T(8,128)(2,1)S(1)}, u32[]{:S(2)}, u32[]{:S(2)}) %collective-permute-start.5) | collective-permute-done | bytes 213024 | tf_op jit(solution)/shard_map/ppermute | solution.py:264
  100.7 0.7 constant_dynamic-update-slice_fusion.2
  101.4 0.7 constant_dynamic-update-slice_fusion.1
  102.1 0.7 constant_dynamic-update-slice_fusion
  102.8 2.6 %collective-permute-done.8 = bf16[16,104,256]{2,1,0:T(8,128)(2,1)S(1)} collective-permute-done((bf16[16,104,256]{2,1,0:T(8,128)(2,1)}, bf16[16,104,256]{2,1,0:T(8,128)(2,1)S(1)}, u32[]{:S(2)}, u32[]{:S(2)}) %collective-permute-start.8) | collective-permute-done | bytes 852000 | tf_op jit(solution)/shard_map/ppermute | solution.py:268
  105.4 0.1 constant_dynamic-update-slice_fusion.7
  105.5 0.1 fusion.2
  105.6 0.1 add.30.label_ref
  105.7 1.6 %copy-done.1 = bf16[1024,1024]{1,0:T(8,128)(2,1)S(1)} copy-done((bf16[1024,1024]{1,0:T(8,128)(2,1)S(1)}, bf16[1024,1024]{1,0:T(8,128)(2,1)}, u32[]{:S(2)}) %copy-start.1) | copy-done | bytes 2097176
  107.3 1.4 own_query.1
  108.7 3.1 %collective-permute-start.9 = (bf16[96,1024]{1,0:T(8,128)(2,1)S(1)}, bf16[96,1024]{1,0:T(8,128)(2,1)S(1)}, u32[]{:S(2)}, u32[]{:S(2)}) collective-permute-start(bf16[96,1024]{1,0:T(8,128)(2,1)S(1)} %get-tuple-element.26.refs_0_), channel_id=1, source_target_pairs={{0,64},{32,96},{64,0},{96,32},{1,65},{33,97},{65,1},{97,33},{2,66}... | collective-permute-start | bytes 589832 | tf_op jit(solution)/shard_map/ppermute | solution.py:417
  111.8 0.2 collective-permute-start.11
  112.0 3.0 %collective-permute-start.12 = (bf16[96,1024]{1,0:T(8,128)(2,1)S(1)}, bf16[96,1024]{1,0:T(8,128)(2,1)S(1)}, u32[]{:S(2)}, u32[]{:S(2)}) collective-permute-start(bf16[96,1024]{1,0:T(8,128)(2,1)S(1)} %get-tuple-element.26.refs_0_), channel_id=1, source_target_pairs={{0,96},{32,0},{64,32},{96,64},{1,97},{33,1},{65,33},{97,65},{2,98}... | collective-permute-start | bytes 589832 | tf_op jit(solution)/shard_map/ppermute | solution.py:417
  115.1 12.5 %group_keys.1 = (bf16[256,3072]{1,0:T(8,128)(2,1)S(1)}, bf16[3072,256]{1,0:T(8,128)(2,1)S(1)}) custom-call(s32[1,3328]{1,0:T(1,128)S(1)} %add.30.label_ref, bf16[3328,256]{1,0:T(8,128)(2,1)S(1)} %bitcast.13, bf16[256,1024]{1,0:T(8,128)(2,1)S(1)} %copy-done.3, f32[1,1024]{1,0:T(1,128)S(1)} %bitcast.18, bf16[1024,256]{1,0:T(8,128)(2,1)S(1)} %copy-done.5, ...), custom_call_target="tpu_custom_call" | custom-call | tf_op jit(solution)/shard_map/group_keys/pallas_call | solution.py:422
  127.5 3.4 %attend.3 = bf16[96,1408]{1,0:T(8,128)(2,1)S(1)} custom-call(f32[8]{0:T(128)S(1)} %broadcast_multiply_fusion.factor_ref, bf16[256,3072]{1,0:T(8,128)(2,1)S(1)} %get-tuple-element.24.key_ref, bf16[3072,256]{1,0:T(8,128)(2,1)S(1)} %get-tuple-element.25.value_ref, bf16[96,1024]{1,0:T(8,128)(2,1)S(1)} %collective-permute-done.9.refs_0_), custom_call_target="tpu_custom_call" | custom-call | tf_op jit(solution)/shard_map/attend/pallas_call | solution.py:435
  130.9 1.1 collective-permute-start.10
  132.0 5.9 %attend.4 = (bf16[96,1408]{1,0:T(8,128)(2,1)S(1)}, bf16[96,1408]{1,0:T(8,128)(2,1)S(1)}) custom-call(f32[8]{0:T(128)S(1)} %broadcast_multiply_fusion.factor_ref, bf16[256,3072]{1,0:T(8,128)(2,1)S(1)} %get-tuple-element.24.key_ref, bf16[3072,256]{1,0:T(8,128)(2,1)S(1)} %get-tuple-element.25.value_ref, bf16[96,1024]{1,0:T(8,128)(2,1)S(1)} %collective-permute-done.11.refs_0_, ...), custom_call_target="tpu_custom_call" | custom-call | tf_op jit(solution)/shard_map/attend/pallas_call | solution.py:435
  138.0 0.7 collective-permute-start.13
  138.7 1.4 collective-permute-start.14
  140.0 3.4 %attend.5.d_ref = bf16[96,1408]{1,0:T(8,128)(2,1)S(1)} custom-call(f32[8]{0:T(128)S(1)} %broadcast_multiply_fusion.factor_ref, bf16[256,3072]{1,0:T(8,128)(2,1)S(1)} %get-tuple-element.24.key_ref, bf16[3072,256]{1,0:T(8,128)(2,1)S(1)} %get-tuple-element.25.value_ref, bf16[96,1024]{1,0:T(8,128)(2,1)S(1)} %get-tuple-element.26.refs_0_), custom_call_target="tpu_custom_call" | custom-call | tf_op jit(solution)/shard_map/attend/pallas_call | solution.py:435
  143.4 2.3 %collective-permute-done.13.b_ref = bf16[96,1408]{1,0:T(8,128)(2,1)S(1)} collective-permute-done((bf16[96,1408]{1,0:T(8,128)(2,1)S(1)}, bf16[96,1408]{1,0:T(8,128)(2,1)S(1)}, u32[]{:S(2)}, u32[]{:S(2)}) %collective-permute-start.13) | collective-permute-done | bytes 270368 | tf_op jit(solution)/shard_map/ppermute | solution.py:444
  145.7 1.6 %collective-permute-done.14.c_ref = bf16[96,1408]{1,0:T(8,128)(2,1)S(1)} collective-permute-done((bf16[96,1408]{1,0:T(8,128)(2,1)S(1)}, bf16[96,1408]{1,0:T(8,128)(2,1)S(1)}, u32[]{:S(2)}, u32[]{:S(2)}) %collective-permute-start.14) | collective-permute-done | bytes 270368 | tf_op jit(solution)/shard_map/ppermute | solution.py:444
  147.3 1.7 %merge.1 = bf16[96,1024]{1,0:T(8,128)(2,1)} custom-call(bf16[96,1408]{1,0:T(8,128)(2,1)S(1)} %collective-permute-done.10.a_ref, bf16[96,1408]{1,0:T(8,128)(2,1)S(1)} %collective-permute-done.13.b_ref, bf16[96,1408]{1,0:T(8,128)(2,1)S(1)} %collective-permute-done.14.c_ref, bf16[96,1408]{1,0:T(8,128)(2,1)S(1)} %attend.5.d_ref, ...), custom_call_target="tpu_custom_call" | custom-call | tf_op jit(solution)/shard_map/merge/pallas_call | solution.py:445
  (40 shorter events, 0.1 us)
Async XLA Ops:
  1.3 1.9 %copy-start = (bf16[6144,256]{1,0:T(8,128)(2,1)S(1)}, bf16[6144,256]{1,0:T(8,128)(2,1)}, u32[]{:S(2)}) copy-start(bf16[6144,256]{1,0:T(8,128)(2,1)} %own_ref.3) | copy-start | bytes 9437188
  3.2 10.2 %copy-start.7 = (s32[1,36864]{1,0:T(1,128)S(1)}, s32[1,36864]{1,0:T(1,128)}, u32[]{:S(2)}) copy-start(s32[1,36864]{1,0:T(1,128)} %param.20) | copy-start | bytes 442372
  3.2 10.2 %copy-start.8 = (s32[1,36864]{1,0:T(1,128)S(1)}, s32[1,36864]{1,0:T(1,128)}, u32[]{:S(2)}) copy-start(s32[1,36864]{1,0:T(1,128)} %param.21) | copy-start | bytes 442372
  3.2 23.8 %copy-start.14 = (s32[1,97]{1,0:T(1,128)S(1)}, s32[1,97]{1,0:T(1,128)}, u32[]{:S(2)}) copy-start(s32[1,97]{1,0:T(1,128)} %param.23) | copy-start | bytes 1168
  5.1 22.6 %collective-permute-start = (bf16[256,256]{1,0:T(8,128)(2,1)S(1)}, bf16[256,256]{1,0:T(8,128)(2,1)S(1)}, u32[]{:S(2)}, u32[]{:S(2)}) collective-permute-start(bf16[256,256]{1,0:T(8,128)(2,1)S(1)} %get-tuple-element.18), channel_id=1, source_target_pairs={{0,1},{1,2},{2,3},{3,4},{4,5},{5,6},{6,7},{7,8},{8,9},{9,10},{10,1... | collective-permute-start | bytes 393224 | tf_op jit(solution)/shard_map/ppermute | solution.py:396
  5.1 22.5 %collective-permute-start.1 = (bf16[256,256]{1,0:T(8,128)(2,1)S(1)}, bf16[256,256]{1,0:T(8,128)(2,1)S(1)}, u32[]{:S(2)}, u32[]{:S(2)}) collective-permute-start(bf16[256,256]{1,0:T(8,128)(2,1)S(1)} %get-tuple-element.19), channel_id=1, source_target_pairs={{0,127},{1,0},{2,1},{3,2},{4,3},{5,4},{6,5},{7,6},{8,7},{9,8},{10,... | collective-permute-start | bytes 393224 | tf_op jit(solution)/shard_map/ppermute | solution.py:397
  24.3 0.7 copy-start.9
  24.9 2.8 %copy-start.4 = (s32[2,144,128]{2,1,0:T(8,128)}, s32[2,144,128]{2,1,0:T(8,128)S(1)}, u32[]{:S(2)}) copy-start(s32[2,144,128]{2,1,0:T(8,128)S(1)} %get-tuple-element.17.local_ref) | copy-start | bytes 442372
  25.0 2.7 %copy-start.13 = (s32[144]{0:T(256)}, s32[144]{0:T(256)S(1)}, u32[]{:S(2)}) copy-start(s32[144]{0:T(256)S(1)} %minimum_reduce_fusion.start_ref) | copy-start | bytes 1732
  27.7 0.6 copy-start.11
  27.7 0.7 copy-start.12
  78.4 7.5 %collective-permute-start.2 = (bf16[1,104,256]{2,1,0:T(8,128)(2,1)}, bf16[1,104,256]{2,1,0:T(8,128)(2,1)S(1)}, u32[]{:S(2)}, u32[]{:S(2)}) collective-permute-start(bf16[1,104,256]{2,1,0:T(8,128)(2,1)} %bitcast.19), channel_id=1, source_target_pairs={{0,2},{1,3},{2,4},{3,5},{4,6},{5,7},{6,0},{7,1},{8,10},{9,11},{10,... | collective-permute-start | bytes 159752 | tf_op jit(solution)/shard_map/ppermute | solution.py:261
  78.4 7.5 %collective-permute-start.3 = (bf16[1,104,256]{2,1,0:T(8,128)(2,1)}, bf16[1,104,256]{2,1,0:T(8,128)(2,1)S(1)}, u32[]{:S(2)}, u32[]{:S(2)}) collective-permute-start(bf16[1,104,256]{2,1,0:T(8,128)(2,1)} %bitcast.20), channel_id=1, source_target_pairs={{0,6},{1,7},{2,0},{3,1},{4,2},{5,3},{6,4},{7,5},{8,14},{9,15},{10,... | collective-permute-start | bytes 159752 | tf_op jit(solution)/shard_map/ppermute | solution.py:261
  83.0 5.8 %collective-permute-start.4 = (bf16[1,104,256]{2,1,0:T(8,128)(2,1)}, bf16[1,104,256]{2,1,0:T(8,128)(2,1)S(1)}, u32[]{:S(2)}, u32[]{:S(2)}) collective-permute-start(bf16[1,104,256]{2,1,0:T(8,128)(2,1)} %bitcast.21), channel_id=1, source_target_pairs={{0,4},{1,5},{2,6},{3,7},{4,0},{5,1},{6,2},{7,3},{8,12},{9,13},{10,... | collective-permute-start | bytes 159752 | tf_op jit(solution)/shard_map/ppermute | solution.py:261
  89.7 10.9 %collective-permute-start.5 = (bf16[4,104,256]{2,1,0:T(8,128)(2,1)S(1)}, bf16[4,104,256]{2,1,0:T(8,128)(2,1)S(1)}, u32[]{:S(2)}, u32[]{:S(2)}) collective-permute-start(bf16[4,104,256]{2,1,0:T(8,128)(2,1)S(1)} %pad_maximum_fusion), channel_id=1, source_target_pairs={{0,8},{1,9},{2,10},{3,11},{4,12},{5,13},{6,14},{7,15},{8,16},{9,17... | collective-permute-start | bytes 638984 | tf_op jit(solution)/shard_map/ppermute | solution.py:264
  91.3 10.1 %collective-permute-start.6 = (bf16[4,104,256]{2,1,0:T(8,128)(2,1)S(1)}, bf16[4,104,256]{2,1,0:T(8,128)(2,1)S(1)}, u32[]{:S(2)}, u32[]{:S(2)}) collective-permute-start(bf16[4,104,256]{2,1,0:T(8,128)(2,1)S(1)} %pad_maximum_fusion), channel_id=1, source_target_pairs={{0,24},{1,25},{2,26},{3,27},{4,28},{5,29},{6,30},{7,31},{8,0},{9,1... | collective-permute-start | bytes 638984 | tf_op jit(solution)/shard_map/ppermute | solution.py:264
  93.0 9.1 %collective-permute-start.7 = (bf16[4,104,256]{2,1,0:T(8,128)(2,1)S(1)}, bf16[4,104,256]{2,1,0:T(8,128)(2,1)S(1)}, u32[]{:S(2)}, u32[]{:S(2)}) collective-permute-start(bf16[4,104,256]{2,1,0:T(8,128)(2,1)S(1)} %pad_maximum_fusion), channel_id=1, source_target_pairs={{0,16},{1,17},{2,18},{3,19},{4,20},{5,21},{6,22},{7,23},{8,24},{9,... | collective-permute-start | bytes 638984 | tf_op jit(solution)/shard_map/ppermute | solution.py:264
  100.7 5.0 %copy-start.3 = (bf16[256,1024]{1,0:T(8,128)(2,1)S(1)}, bf16[256,1024]{1,0:T(8,128)(2,1)}, u32[]{:S(2)}) copy-start(bf16[256,1024]{1,0:T(8,128)(2,1)} %w_pool_ref.3) | copy-start | bytes 1572868
  100.7 5.0 %copy-start.10 = (f32[1024]{0:T(1024)S(1)}, f32[1024]{0:T(1024)}, u32[]{:S(2)}) copy-start(f32[1024]{0:T(1024)} %param.30) | copy-start | bytes 12292
  102.8 2.6 %collective-permute-start.8 = (bf16[16,104,256]{2,1,0:T(8,128)(2,1)}, bf16[16,104,256]{2,1,0:T(8,128)(2,1)S(1)}, u32[]{:S(2)}, u32[]{:S(2)}) collective-permute-start(bf16[16,104,256]{2,1,0:T(8,128)(2,1)} %get-tuple-element.30), channel_id=1, source_target_pairs={{0,1},{1,0},{2,3},{3,2},{4,5},{5,4},{6,7},{7,6},{8,9},{9,8},{10,11... | collective-permute-start | bytes 2555912 | tf_op jit(solution)/shard_map/ppermute | solution.py:268
  105.7 1.6 %copy-start.1 = (bf16[1024,1024]{1,0:T(8,128)(2,1)S(1)}, bf16[1024,1024]{1,0:T(8,128)(2,1)}, u32[]{:S(2)}) copy-start(bf16[1024,1024]{1,0:T(8,128)(2,1)} %w_query_ref.1) | copy-start | bytes 6291460
  107.3 7.8 %copy-start.15 = (f32[8]{0:T(128)S(1)}, f32[8]{0:T(128)}, u32[]{:S(2)}) copy-start(f32[8]{0:T(128)} %param.35) | copy-start | bytes 100
  107.3 7.8 %copy-start.5 = (bf16[1024,256]{1,0:T(8,128)(2,1)S(1)}, bf16[1024,256]{1,0:T(8,128)(2,1)}, u32[]{:S(2)}) copy-start(bf16[1024,256]{1,0:T(8,128)(2,1)} %w_key_ref.1) | copy-start | bytes 1572868
  107.3 7.8 %copy-start.6 = (bf16[1024,256]{1,0:T(8,128)(2,1)S(1)}, bf16[1024,256]{1,0:T(8,128)(2,1)}, u32[]{:S(2)}) copy-start(bf16[1024,256]{1,0:T(8,128)(2,1)} %w_value_ref.1) | copy-start | bytes 1572868
  108.7 18.8 %collective-permute-start.9 = (bf16[96,1024]{1,0:T(8,128)(2,1)S(1)}, bf16[96,1024]{1,0:T(8,128)(2,1)S(1)}, u32[]{:S(2)}, u32[]{:S(2)}) collective-permute-start(bf16[96,1024]{1,0:T(8,128)(2,1)S(1)} %get-tuple-element.26.refs_0_), channel_id=1, source_target_pairs={{0,64},{32,96},{64,0},{96,32},{1,65},{33,97},{65,1},{97,33},{2,66}... | collective-permute-start | bytes 589832 | tf_op jit(solution)/shard_map/ppermute | solution.py:417
  111.8 20.2 %collective-permute-start.11 = (bf16[96,1024]{1,0:T(8,128)(2,1)S(1)}, bf16[96,1024]{1,0:T(8,128)(2,1)S(1)}, u32[]{:S(2)}, u32[]{:S(2)}) collective-permute-start(bf16[96,1024]{1,0:T(8,128)(2,1)S(1)} %get-tuple-element.26.refs_0_), channel_id=1, source_target_pairs={{0,32},{32,64},{64,96},{96,0},{1,33},{33,65},{65,97},{97,1},{2,34}... | collective-permute-start | bytes 589832 | tf_op jit(solution)/shard_map/ppermute | solution.py:417
  112.0 20.1 %collective-permute-start.12 = (bf16[96,1024]{1,0:T(8,128)(2,1)S(1)}, bf16[96,1024]{1,0:T(8,128)(2,1)S(1)}, u32[]{:S(2)}, u32[]{:S(2)}) collective-permute-start(bf16[96,1024]{1,0:T(8,128)(2,1)S(1)} %get-tuple-element.26.refs_0_), channel_id=1, source_target_pairs={{0,96},{32,0},{64,32},{96,64},{1,97},{33,1},{65,33},{97,65},{2,98}... | collective-permute-start | bytes 589832 | tf_op jit(solution)/shard_map/ppermute | solution.py:417
  130.9 12.5 %collective-permute-start.10 = (bf16[96,1408]{1,0:T(8,128)(2,1)S(1)}, bf16[96,1408]{1,0:T(8,128)(2,1)S(1)}, u32[]{:S(2)}, u32[]{:S(2)}) collective-permute-start(bf16[96,1408]{1,0:T(8,128)(2,1)S(1)} %attend.3), channel_id=1, source_target_pairs={{0,64},{32,96},{64,0},{96,32},{1,65},{33,97},{65,1},{97,33},{2,66}... | collective-permute-start | bytes 811016 | tf_op jit(solution)/shard_map/ppermute | solution.py:444
  138.0 7.8 %collective-permute-start.13 = (bf16[96,1408]{1,0:T(8,128)(2,1)S(1)}, bf16[96,1408]{1,0:T(8,128)(2,1)S(1)}, u32[]{:S(2)}, u32[]{:S(2)}) collective-permute-start(bf16[96,1408]{1,0:T(8,128)(2,1)S(1)} %get-tuple-element.27), channel_id=1, source_target_pairs={{0,96},{32,0},{64,32},{96,64},{1,97},{33,1},{65,33},{97,65},{2,98}... | collective-permute-start | bytes 811016 | tf_op jit(solution)/shard_map/ppermute | solution.py:444
  138.6 8.6 %copy-start.2 = (bf16[1024,1024]{1,0:T(8,128)(2,1)S(1)}, bf16[1024,1024]{1,0:T(8,128)(2,1)}, u32[]{:S(2)}) copy-start(bf16[1024,1024]{1,0:T(8,128)(2,1)} %w_out_ref.1) | copy-start | bytes 6291460
  138.7 8.6 %collective-permute-start.14 = (bf16[96,1408]{1,0:T(8,128)(2,1)S(1)}, bf16[96,1408]{1,0:T(8,128)(2,1)S(1)}, u32[]{:S(2)}, u32[]{:S(2)}) collective-permute-start(bf16[96,1408]{1,0:T(8,128)(2,1)S(1)} %get-tuple-element.28), channel_id=1, source_target_pairs={{0,32},{32,64},{64,96},{96,0},{1,33},{33,65},{65,97},{97,1},{2,34}... | collective-permute-start | bytes 811016 | tf_op jit(solution)/shard_map/ppermute | solution.py:444
where the time goes:
time: 150 us; the launch traced here: 149 us
  Pallas kernels  91 us (61%)
  starting transfers between devices  28.9 us (19%)
  waiting for transfers between devices  13.5 us (9%)
  local copies, waits for them, and re-layouts  11.7 us (8%)
  other arithmetic  2.37 us (2%)
  between operations  1.51 us (1%)
    pallas_call x1, Pallas kernels, fine_pass(): pl.pallas_call(fine_kernel, out_shape=(jax.ShapeDtypeStruct(own.shape, bf...  50.1 us
    pallas_call x3, Pallas kernels, body(): pl.pallas_call(attend_kernel, out_shape=[jax.ShapeDtypeStruct((par_dev, w...  12.7 us
    pallas_call x1, Pallas kernels, body(): pl.pallas_call(key_kernel, out_shape=(jax.ShapeDtypeStruct((256, known),...  12.5 us
    pallas_call x1, Pallas kernels, sorted_edges(): pl.pallas_call(sort_kernel, out_shape=(shape, shape), scratch_shapes=[plt...  10.8 us
    unnamed x38, local copies, waits for them, and re-layouts  9.59 us
    ppermute x1, starting transfers between devices, body(): lax.ppermute(to_prev, both, [(i, (i - 1) % every) for i in range(every)])  8.27 us
    ppermute x3, starting transfers between devices, body(): lax.ppermute(query, 'grp', [(i, (i + by) % groups) for i in range(groups)])  6.3 us
    ppermute x3, starting transfers between devices, along_z(): lax.ppermute(value, 'cur', [(i, i // 8 * 8 + (i + 2 * by) % 8) for i in r...  6.01 us
  transfers between devices with their start and end apart: 15, of which 5 were waited for; matrix products, arithmetic and copies ran while one was open for 5% of the time, Pallas kernels for 24%

commit v1 on v0

--- a/solution.py
+++ b/solution.py
@@ -414,7 +414,7 @@
         name="own_query",
     )((lax.axis_index("cur") * par_dev)[None], labels, rows, w_pool, gain, w_query)
     query, rows = lax.optimization_barrier((query, rows))
-    asked = {by: lax.ppermute(query, "grp", [(i, (i + by) % groups) for i in range(groups)]) for by in (2, 1, 3)}
+    asked = {by: lax.ppermute(query, "grp", [(i, (i + by) % groups) for i in range(groups)]) for by in (1, 3, 2)}
     asked[0] = query
     known = par_dev * devices
     step = 768
@@ -431,7 +431,7 @@
     )(labels, rows, w_pool, gain, w_key, w_value)
     factor = head_scale * (math.log2(math.e) / math.sqrt(128.0))
     found = []
-    for shifts in ((2,), (1, 3), (0,)):
+    for shifts in ((1, 3), (2,), (0,)):
         pieces = pl.pallas_call(
             attend_kernel,
             out_shape=[jax.ShapeDtypeStruct((par_dev, width + 384), bf16) for by in shifts],

time: 150 us -> 151 us (level)
  Pallas kernels: 91 us -> 93.2 us
  starting transfers between devices: 28.9 us -> 27.3 us
    ppermute x3, starting transfers between devices: 6.01 us -> 3.24 us  [along_z(): lax.ppermute(value, 'cur', [(i, i // 8 * 8 + (i + 2 * by) % 8) for i in r...]
    pallas_call x1, Pallas kernels: 50.1 us -> 52.3 us  [fine_pass(): pl.pallas_call(fine_kernel, out_shape=(jax.ShapeDtypeStruct(own.shape, bf...]
  transfers between devices with their start and end apart: 15 -> 15, of which waited for: 5 -> 7; matrix products, arithmetic and copies ran while one was open for 5% -> 5% of each run, Pallas kernels for 24% -> 24%
where the time goes in v1:
time: 151 us
  Pallas kernels  93.2 us (62%)
  starting transfers between devices  27.3 us (18%)
  waiting for transfers between devices  14.4 us (10%)
  local copies, waits for them, and re-layouts  11.8 us (8%)
  other arithmetic  2.37 us (2%)
  between operations  1.53 us (1%)
    pallas_call x1, Pallas kernels, fine_pass(): pl.pallas_call(fine_kernel, out_shape=(jax.ShapeDtypeStruct(own.shape, bf...  52.3 us
    pallas_call x3, Pallas kernels, body(): pl.pallas_call(attend_kernel, out_shape=[jax.ShapeDtypeStruct((par_dev, w...  12.7 us
    pallas_call x1, Pallas kernels, body(): pl.pallas_call(key_kernel, out_shape=(jax.ShapeDtypeStruct((256, known),...  12.5 us
    pallas_call x1, Pallas kernels, sorted_edges(): pl.pallas_call(sort_kernel, out_shape=(shape, shape), scratch_shapes=[plt...  10.8 us
    unnamed x38, local copies, waits for them, and re-layouts  9.62 us
    ppermute x1, starting transfers between devices, body(): lax.ppermute(to_prev, both, [(i, (i - 1) % every) for i in range(every)])  8.27 us
    ppermute x3, starting transfers between devices, body(): lax.ppermute(query, 'grp', [(i, (i + by) % groups) for i in range(groups)])  6.94 us
    ppermute x3, starting transfers between devices, body(): lax.ppermute(piece, 'grp', [(i, (i - by) % groups) for i in range(groups)])  4.58 us
  transfers between devices with their start and end apart: 15, of which 7 were waited for; matrix products, arithmetic and copies ran while one was open for 5% of the time, Pallas kernels for 24%

profile of v1, /device:TPU:0, one launch (start us, length us, event | category | flops | bytes accessed | tf_op | source)
XLA Modules:
  0.0 150.6 jit_solution(9205496258885113279)
XLA Ops:
  0.6 0.7 reshape.60.index_ref
  1.3 1.9 %copy-done = bf16[6144,256]{1,0:T(8,128)(2,1)S(1)} copy-done((bf16[6144,256]{1,0:T(8,128)(2,1)S(1)}, bf16[6144,256]{1,0:T(8,128)(2,1)}, u32[]{:S(2)}) %copy-start) | copy-done | bytes 3145752
  3.2 1.8 %halo_cells.1 = (bf16[256,256]{1,0:T(8,128)(2,1)S(1)}, bf16[256,256]{1,0:T(8,128)(2,1)S(1)}) custom-call(s32[4,128]{1,0:T(4,128)S(1)} %reshape.60.index_ref, bf16[6144,256]{1,0:T(8,128)(2,1)S(1)} %copy-done), custom_call_target="tpu_custom_call" | custom-call | tf_op jit(solution)/shard_map/halo_cells/pallas_call | solution.py:388
  5.1 0.1 collective-permute-start
  5.1 8.3 %collective-permute-start.1 = (bf16[256,256]{1,0:T(8,128)(2,1)S(1)}, bf16[256,256]{1,0:T(8,128)(2,1)S(1)}, u32[]{:S(2)}, u32[]{:S(2)}) collective-permute-start(bf16[256,256]{1,0:T(8,128)(2,1)S(1)} %get-tuple-element.19), channel_id=1, source_target_pairs={{0,127},{1,0},{2,1},{3,2},{4,3},{5,4},{6,5},{7,6},{8,7},{9,8},{10,... | collective-permute-start | bytes 393224 | tf_op jit(solution)/shard_map/ppermute | solution.py:397
  13.4 10.8 %sort_edges.1 = (s32[2,144,128]{2,1,0:T(8,128)S(1)}, s32[2,144,128]{2,1,0:T(8,128)S(1)}) custom-call(s32[36,8,128]{2,1,0:T(8,128)S(1)} %bitcast.14, s32[36,8,128]{2,1,0:T(8,128)S(1)} %bitcast.15), custom_call_target="tpu_custom_call" | custom-call | tf_op jit(solution)/shard_map/sort_edges/pallas_call | solution.py:90
  24.3 0.7 copy-done.9
  24.9 0.1 minimum_reduce_fusion.start_ref
  25.1 0.1 fusion
  25.2 1.2 fusion.4
  27.1 0.6 pad.4.parent_ref
  27.7 0.6 copy-done.11
  28.4 52.3 %fine_cells.1 = (bf16[6144,256]{1,0:T(8,128)(2,1)}, bf16[104,256]{1,0:T(8,128)(2,1)}) custom-call(s32[36864]{0:T(1024)} %bitcast.16, s32[144]{0:T(256)} %copy-done.13, s32[144]{0:T(256)} %get-tuple-element.45.windows_ref, s32[1]{0:T(128)} %bitcast.3.pairs_ref, s32[2,144,128]{2,1,0:T(8,128)} %copy-done.4, s32[24,1,256]{2,1,0:T(1,128)} %bitcast.23, ...), custom_call_target="tpu_custom_call" | custom-call | tf_op jit(solution)/shard_map/fine_cells/pallas_call | solution.py:230
  80.7 0.1 collective-permute-start.2
  80.8 3.2 %collective-permute-start.3 = (bf16[1,104,256]{2,1,0:T(8,128)(2,1)}, bf16[1,104,256]{2,1,0:T(8,128)(2,1)S(1)}, u32[]{:S(2)}, u32[]{:S(2)}) collective-permute-start(bf16[1,104,256]{2,1,0:T(8,128)(2,1)} %bitcast.20), channel_id=1, source_target_pairs={{0,6},{1,7},{2,0},{3,1},{4,2},{5,3},{6,4},{7,5},{8,14},{9,15},{10,... | collective-permute-start | bytes 159752 | tf_op jit(solution)/shard_map/ppermute | solution.py:261
  83.9 1.5 constant_dynamic-update-slice_fusion.6
  85.4 0.8 collective-permute-done.2
  86.2 3.5 %collective-permute-done.4 = bf16[1,104,256]{2,1,0:T(8,128)(2,1)S(1)} collective-permute-done((bf16[1,104,256]{2,1,0:T(8,128)(2,1)}, bf16[1,104,256]{2,1,0:T(8,128)(2,1)S(1)}, u32[]{:S(2)}, u32[]{:S(2)}) %collective-permute-start.4) | collective-permute-done | bytes 53280 | tf_op jit(solution)/shard_map/ppermute | solution.py:261
  89.8 0.8 pad_maximum_fusion
  90.6 0.1 collective-permute-start.5
  90.7 3.2 %collective-permute-start.6 = (bf16[4,104,256]{2,1,0:T(8,128)(2,1)S(1)}, bf16[4,104,256]{2,1,0:T(8,128)(2,1)S(1)}, u32[]{:S(2)}, u32[]{:S(2)}) collective-permute-start(bf16[4,104,256]{2,1,0:T(8,128)(2,1)S(1)} %pad_maximum_fusion), channel_id=1, source_target_pairs={{0,24},{1,25},{2,26},{3,27},{4,28},{5,29},{6,30},{7,31},{8,0},{9,1... | collective-permute-start | bytes 638984 | tf_op jit(solution)/shard_map/ppermute | solution.py:264
  93.9 0.9 collective-permute-start.7
  94.8 0.6 constant_dynamic-update-slice_fusion.5
  95.4 0.6 constant_dynamic-update-slice_fusion.4
  96.0 0.6 constant_dynamic-update-slice_fusion.3
  96.7 1.7 %collective-permute-done.5 = bf16[4,104,256]{2,1,0:T(8,128)(2,1)S(1)} collective-permute-done((bf16[4,104,256]{2,1,0:T(8,128)(2,1)S(1)}, bf16[4,104,256]{2,1,0:T(8,128)(2,1)S(1)}, u32[]{:S(2)}, u32[]{:S(2)}) %collective-permute-start.5) | collective-permute-done | bytes 213024 | tf_op jit(solution)/shard_map/ppermute | solution.py:264
  98.3 0.7 constant_dynamic-update-slice_fusion.2
  99.0 0.5 collective-permute-done.6
  99.6 0.7 constant_dynamic-update-slice_fusion.1
  100.3 1.0 collective-permute-done.7
  101.3 0.7 constant_dynamic-update-slice_fusion
  102.0 2.6 %collective-permute-done.8 = bf16[16,104,256]{2,1,0:T(8,128)(2,1)S(1)} collective-permute-done((bf16[16,104,256]{2,1,0:T(8,128)(2,1)}, bf16[16,104,256]{2,1,0:T(8,128)(2,1)S(1)}, u32[]{:S(2)}, u32[]{:S(2)}) %collective-permute-start.8) | collective-permute-done | bytes 852000 | tf_op jit(solution)/shard_map/ppermute | solution.py:268
  104.6 0.1 fusion.2
  104.7 0.1 add.30.label_ref
  104.9 1.6 %copy-done.1 = bf16[1024,1024]{1,0:T(8,128)(2,1)S(1)} copy-done((bf16[1024,1024]{1,0:T(8,128)(2,1)S(1)}, bf16[1024,1024]{1,0:T(8,128)(2,1)}, u32[]{:S(2)}) %copy-start.1) | copy-done | bytes 2097176
  106.4 1.4 own_query.1
  107.9 0.4 collective-permute-start.9
  108.3 5.1 %collective-permute-start.10 = (bf16[96,1024]{1,0:T(8,128)(2,1)S(1)}, bf16[96,1024]{1,0:T(8,128)(2,1)S(1)}, u32[]{:S(2)}, u32[]{:S(2)}) collective-permute-start(bf16[96,1024]{1,0:T(8,128)(2,1)S(1)} %get-tuple-element.26.refs_0_), channel_id=1, source_target_pairs={{0,96},{32,0},{64,32},{96,64},{1,97},{33,1},{65,33},{97,65},{2,98}... | collective-permute-start | bytes 589832 | tf_op jit(solution)/shard_map/ppermute | solution.py:417
  113.5 1.4 collective-permute-start.13
  114.9 12.5 %group_keys.1 = (bf16[256,3072]{1,0:T(8,128)(2,1)S(1)}, bf16[3072,256]{1,0:T(8,128)(2,1)S(1)}) custom-call(s32[1,3328]{1,0:T(1,128)S(1)} %add.30.label_ref, bf16[3328,256]{1,0:T(8,128)(2,1)S(1)} %bitcast.13, bf16[256,1024]{1,0:T(8,128)(2,1)S(1)} %copy-done.3, f32[1,1024]{1,0:T(1,128)S(1)} %bitcast.18, bf16[1024,256]{1,0:T(8,128)(2,1)S(1)} %copy-done.5, ...), custom_call_target="tpu_custom_call" | custom-call | tf_op jit(solution)/shard_map/group_keys/pallas_call | solution.py:422
  127.4 5.9 %attend.3 = (bf16[96,1408]{1,0:T(8,128)(2,1)S(1)}, bf16[96,1408]{1,0:T(8,128)(2,1)S(1)}) custom-call(f32[8]{0:T(128)S(1)} %broadcast_multiply_fusion.factor_ref, bf16[256,3072]{1,0:T(8,128)(2,1)S(1)} %get-tuple-element.24.key_ref, bf16[3072,256]{1,0:T(8,128)(2,1)S(1)} %get-tuple-element.25.value_ref, bf16[96,1024]{1,0:T(8,128)(2,1)S(1)} %collective-permute-done.9.refs_0_, ...), custom_call_target="tpu_custom_call" | custom-call | tf_op jit(solution)/shard_map/attend/pallas_call | solution.py:435
  133.3 0.6 collective-permute-start.11
  133.9 1.4 collective-permute-start.12
  135.4 3.4 %attend.4 = bf16[96,1408]{1,0:T(8,128)(2,1)S(1)} custom-call(f32[8]{0:T(128)S(1)} %broadcast_multiply_fusion.factor_ref, bf16[256,3072]{1,0:T(8,128)(2,1)S(1)} %get-tuple-element.24.key_ref, bf16[3072,256]{1,0:T(8,128)(2,1)S(1)} %get-tuple-element.25.value_ref, bf16[96,1024]{1,0:T(8,128)(2,1)S(1)} %collective-permute-done.13.refs_0_), custom_call_target="tpu_custom_call" | custom-call | tf_op jit(solution)/shard_map/attend/pallas_call | solution.py:435
  138.8 2.5 %collective-permute-start.14 = (bf16[96,1408]{1,0:T(8,128)(2,1)S(1)}, bf16[96,1408]{1,0:T(8,128)(2,1)S(1)}, u32[]{:S(2)}, u32[]{:S(2)}) collective-permute-start(bf16[96,1408]{1,0:T(8,128)(2,1)S(1)} %attend.4), channel_id=1, source_target_pairs={{0,64},{32,96},{64,0},{96,32},{1,65},{33,97},{65,1},{97,33},{2,66}... | collective-permute-start | bytes 811016 | tf_op jit(solution)/shard_map/ppermute | solution.py:444
  141.2 3.4 %attend.5.d_ref = bf16[96,1408]{1,0:T(8,128)(2,1)S(1)} custom-call(f32[8]{0:T(128)S(1)} %broadcast_multiply_fusion.factor_ref, bf16[256,3072]{1,0:T(8,128)(2,1)S(1)} %get-tuple-element.24.key_ref, bf16[3072,256]{1,0:T(8,128)(2,1)S(1)} %get-tuple-element.25.value_ref, bf16[96,1024]{1,0:T(8,128)(2,1)S(1)} %get-tuple-element.26.refs_0_), custom_call_target="tpu_custom_call" | custom-call | tf_op jit(solution)/shard_map/attend/pallas_call | solution.py:435
  144.7 4.3 %collective-permute-done.14.c_ref = bf16[96,1408]{1,0:T(8,128)(2,1)S(1)} collective-permute-done((bf16[96,1408]{1,0:T(8,128)(2,1)S(1)}, bf16[96,1408]{1,0:T(8,128)(2,1)S(1)}, u32[]{:S(2)}, u32[]{:S(2)}) %collective-permute-start.14) | collective-permute-done | bytes 270368 | tf_op jit(solution)/shard_map/ppermute | solution.py:444
  149.0 1.7 %merge.1 = bf16[96,1024]{1,0:T(8,128)(2,1)} custom-call(bf16[96,1408]{1,0:T(8,128)(2,1)S(1)} %collective-permute-done.11.a_ref, bf16[96,1408]{1,0:T(8,128)(2,1)S(1)} %collective-permute-done.12.b_ref, bf16[96,1408]{1,0:T(8,128)(2,1)S(1)} %collective-permute-done.14.c_ref, bf16[96,1408]{1,0:T(8,128)(2,1)S(1)} %attend.5.d_ref, ...), custom_call_target="tpu_custom_call" | custom-call | tf_op jit(solution)/shard_map/merge/pallas_call | solution.py:445
  (40 shorter events, 0.2 us)
Async XLA Ops:
  1.3 1.9 %copy-start = (bf16[6144,256]{1,0:T(8,128)(2,1)S(1)}, bf16[6144,256]{1,0:T(8,128)(2,1)}, u32[]{:S(2)}) copy-start(bf16[6144,256]{1,0:T(8,128)(2,1)} %own_ref.3) | copy-start | bytes 9437188
  3.2 10.2 %copy-start.7 = (s32[1,36864]{1,0:T(1,128)S(1)}, s32[1,36864]{1,0:T(1,128)}, u32[]{:S(2)}) copy-start(s32[1,36864]{1,0:T(1,128)} %param.20) | copy-start | bytes 442372
  3.2 10.2 %copy-start.8 = (s32[1,36864]{1,0:T(1,128)S(1)}, s32[1,36864]{1,0:T(1,128)}, u32[]{:S(2)}) copy-start(s32[1,36864]{1,0:T(1,128)} %param.21) | copy-start | bytes 442372
  3.2 23.8 %copy-start.14 = (s32[1,97]{1,0:T(1,128)S(1)}, s32[1,97]{1,0:T(1,128)}, u32[]{:S(2)}) copy-start(s32[1,97]{1,0:T(1,128)} %param.23) | copy-start | bytes 1168
  5.1 22.6 %collective-permute-start = (bf16[256,256]{1,0:T(8,128)(2,1)S(1)}, bf16[256,256]{1,0:T(8,128)(2,1)S(1)}, u32[]{:S(2)}, u32[]{:S(2)}) collective-permute-start(bf16[256,256]{1,0:T(8,128)(2,1)S(1)} %get-tuple-element.18), channel_id=1, source_target_pairs={{0,1},{1,2},{2,3},{3,4},{4,5},{5,6},{6,7},{7,8},{8,9},{9,10},{10,1... | collective-permute-start | bytes 393224 | tf_op jit(solution)/shard_map/ppermute | solution.py:396
  5.1 22.5 %collective-permute-start.1 = (bf16[256,256]{1,0:T(8,128)(2,1)S(1)}, bf16[256,256]{1,0:T(8,128)(2,1)S(1)}, u32[]{:S(2)}, u32[]{:S(2)}) collective-permute-start(bf16[256,256]{1,0:T(8,128)(2,1)S(1)} %get-tuple-element.19), channel_id=1, source_target_pairs={{0,127},{1,0},{2,1},{3,2},{4,3},{5,4},{6,5},{7,6},{8,7},{9,8},{10,... | collective-permute-start | bytes 393224 | tf_op jit(solution)/shard_map/ppermute | solution.py:397
  24.3 0.7 copy-start.9
  24.9 2.8 %copy-start.4 = (s32[2,144,128]{2,1,0:T(8,128)}, s32[2,144,128]{2,1,0:T(8,128)S(1)}, u32[]{:S(2)}) copy-start(s32[2,144,128]{2,1,0:T(8,128)S(1)} %get-tuple-element.17.local_ref) | copy-start | bytes 442372
  25.0 2.7 %copy-start.13 = (s32[144]{0:T(256)}, s32[144]{0:T(256)S(1)}, u32[]{:S(2)}) copy-start(s32[144]{0:T(256)S(1)} %minimum_reduce_fusion.start_ref) | copy-start | bytes 1732
  27.7 0.6 copy-start.11
  27.7 0.7 copy-start.12
  80.7 5.6 %collective-permute-start.2 = (bf16[1,104,256]{2,1,0:T(8,128)(2,1)}, bf16[1,104,256]{2,1,0:T(8,128)(2,1)S(1)}, u32[]{:S(2)}, u32[]{:S(2)}) collective-permute-start(bf16[1,104,256]{2,1,0:T(8,128)(2,1)} %bitcast.19), channel_id=1, source_target_pairs={{0,2},{1,3},{2,4},{3,5},{4,6},{5,7},{6,0},{7,1},{8,10},{9,11},{10,... | collective-permute-start | bytes 159752 | tf_op jit(solution)/shard_map/ppermute | solution.py:261
  80.8 5.5 %collective-permute-start.3 = (bf16[1,104,256]{2,1,0:T(8,128)(2,1)}, bf16[1,104,256]{2,1,0:T(8,128)(2,1)S(1)}, u32[]{:S(2)}, u32[]{:S(2)}) collective-permute-start(bf16[1,104,256]{2,1,0:T(8,128)(2,1)} %bitcast.20), channel_id=1, source_target_pairs={{0,6},{1,7},{2,0},{3,1},{4,2},{5,3},{6,4},{7,5},{8,14},{9,15},{10,... | collective-permute-start | bytes 159752 | tf_op jit(solution)/shard_map/ppermute | solution.py:261
  83.9 5.8 %collective-permute-start.4 = (bf16[1,104,256]{2,1,0:T(8,128)(2,1)}, bf16[1,104,256]{2,1,0:T(8,128)(2,1)S(1)}, u32[]{:S(2)}, u32[]{:S(2)}) collective-permute-start(bf16[1,104,256]{2,1,0:T(8,128)(2,1)} %bitcast.21), channel_id=1, source_target_pairs={{0,4},{1,5},{2,6},{3,7},{4,0},{5,1},{6,2},{7,3},{8,12},{9,13},{10,... | collective-permute-start | bytes 159752 | tf_op jit(solution)/shard_map/ppermute | solution.py:261
  90.6 7.7 %collective-permute-start.5 = (bf16[4,104,256]{2,1,0:T(8,128)(2,1)S(1)}, bf16[4,104,256]{2,1,0:T(8,128)(2,1)S(1)}, u32[]{:S(2)}, u32[]{:S(2)}) collective-permute-start(bf16[4,104,256]{2,1,0:T(8,128)(2,1)S(1)} %pad_maximum_fusion), channel_id=1, source_target_pairs={{0,8},{1,9},{2,10},{3,11},{4,12},{5,13},{6,14},{7,15},{8,16},{9,17... | collective-permute-start | bytes 638984 | tf_op jit(solution)/shard_map/ppermute | solution.py:264
  90.7 8.9 %collective-permute-start.6 = (bf16[4,104,256]{2,1,0:T(8,128)(2,1)S(1)}, bf16[4,104,256]{2,1,0:T(8,128)(2,1)S(1)}, u32[]{:S(2)}, u32[]{:S(2)}) collective-permute-start(bf16[4,104,256]{2,1,0:T(8,128)(2,1)S(1)} %pad_maximum_fusion), channel_id=1, source_target_pairs={{0,24},{1,25},{2,26},{3,27},{4,28},{5,29},{6,30},{7,31},{8,0},{9,1... | collective-permute-start | bytes 638984 | tf_op jit(solution)/shard_map/ppermute | solution.py:264
  93.9 7.3 %collective-permute-start.7 = (bf16[4,104,256]{2,1,0:T(8,128)(2,1)S(1)}, bf16[4,104,256]{2,1,0:T(8,128)(2,1)S(1)}, u32[]{:S(2)}, u32[]{:S(2)}) collective-permute-start(bf16[4,104,256]{2,1,0:T(8,128)(2,1)S(1)} %pad_maximum_fusion), channel_id=1, source_target_pairs={{0,16},{1,17},{2,18},{3,19},{4,20},{5,21},{6,22},{7,23},{8,24},{9,... | collective-permute-start | bytes 638984 | tf_op jit(solution)/shard_map/ppermute | solution.py:264
  98.3 6.5 %copy-start.3 = (bf16[256,1024]{1,0:T(8,128)(2,1)S(1)}, bf16[256,1024]{1,0:T(8,128)(2,1)}, u32[]{:S(2)}) copy-start(bf16[256,1024]{1,0:T(8,128)(2,1)} %w_pool_ref.3) | copy-start | bytes 1572868
  98.3 6.5 %copy-start.10 = (f32[1024]{0:T(1024)S(1)}, f32[1024]{0:T(1024)}, u32[]{:S(2)}) copy-start(f32[1024]{0:T(1024)} %param.30) | copy-start | bytes 12292
  102.0 2.6 %collective-permute-start.8 = (bf16[16,104,256]{2,1,0:T(8,128)(2,1)}, bf16[16,104,256]{2,1,0:T(8,128)(2,1)S(1)}, u32[]{:S(2)}, u32[]{:S(2)}) collective-permute-start(bf16[16,104,256]{2,1,0:T(8,128)(2,1)} %get-tuple-element.30), channel_id=1, source_target_pairs={{0,1},{1,0},{2,3},{3,2},{4,5},{5,4},{6,7},{7,6},{8,9},{9,8},{10,11... | collective-permute-start | bytes 2555912 | tf_op jit(solution)/shard_map/ppermute | solution.py:268
  104.8 1.6 %copy-start.1 = (bf16[1024,1024]{1,0:T(8,128)(2,1)S(1)}, bf16[1024,1024]{1,0:T(8,128)(2,1)}, u32[]{:S(2)}) copy-start(bf16[1024,1024]{1,0:T(8,128)(2,1)} %w_query_ref.1) | copy-start | bytes 6291460
  106.4 8.4 %copy-start.15 = (f32[8]{0:T(128)S(1)}, f32[8]{0:T(128)}, u32[]{:S(2)}) copy-start(f32[8]{0:T(128)} %param.35) | copy-start | bytes 100
  106.4 8.4 %copy-start.5 = (bf16[1024,256]{1,0:T(8,128)(2,1)S(1)}, bf16[1024,256]{1,0:T(8,128)(2,1)}, u32[]{:S(2)}) copy-start(bf16[1024,256]{1,0:T(8,128)(2,1)} %w_key_ref.1) | copy-start | bytes 1572868
  106.4 8.4 %copy-start.6 = (bf16[1024,256]{1,0:T(8,128)(2,1)S(1)}, bf16[1024,256]{1,0:T(8,128)(2,1)}, u32[]{:S(2)}) copy-start(bf16[1024,256]{1,0:T(8,128)(2,1)} %w_value_ref.1) | copy-start | bytes 1572868
  107.9 19.4 %collective-permute-start.9 = (bf16[96,1024]{1,0:T(8,128)(2,1)S(1)}, bf16[96,1024]{1,0:T(8,128)(2,1)S(1)}, u32[]{:S(2)}, u32[]{:S(2)}) collective-permute-start(bf16[96,1024]{1,0:T(8,128)(2,1)S(1)} %get-tuple-element.26.refs_0_), channel_id=1, source_target_pairs={{0,32},{32,64},{64,96},{96,0},{1,33},{33,65},{65,97},{97,1},{2,34}... | collective-permute-start | bytes 589832 | tf_op jit(solution)/shard_map/ppermute | solution.py:417
  108.3 19.0 %collective-permute-start.10 = (bf16[96,1024]{1,0:T(8,128)(2,1)S(1)}, bf16[96,1024]{1,0:T(8,128)(2,1)S(1)}, u32[]{:S(2)}, u32[]{:S(2)}) collective-permute-start(bf16[96,1024]{1,0:T(8,128)(2,1)S(1)} %get-tuple-element.26.refs_0_), channel_id=1, source_target_pairs={{0,96},{32,0},{64,32},{96,64},{1,97},{33,1},{65,33},{97,65},{2,98}... | collective-permute-start | bytes 589832 | tf_op jit(solution)/shard_map/ppermute | solution.py:417
  113.5 21.9 %collective-permute-start.13 = (bf16[96,1024]{1,0:T(8,128)(2,1)S(1)}, bf16[96,1024]{1,0:T(8,128)(2,1)S(1)}, u32[]{:S(2)}, u32[]{:S(2)}) collective-permute-start(bf16[96,1024]{1,0:T(8,128)(2,1)S(1)} %get-tuple-element.26.refs_0_), channel_id=1, source_target_pairs={{0,64},{32,96},{64,0},{96,32},{1,65},{33,97},{65,1},{97,33},{2,66}... | collective-permute-start | bytes 589832 | tf_op jit(solution)/shard_map/ppermute | solution.py:417
  133.3 11.4 %collective-permute-start.11 = (bf16[96,1408]{1,0:T(8,128)(2,1)S(1)}, bf16[96,1408]{1,0:T(8,128)(2,1)S(1)}, u32[]{:S(2)}, u32[]{:S(2)}) collective-permute-start(bf16[96,1408]{1,0:T(8,128)(2,1)S(1)} %get-tuple-element.27), channel_id=1, source_target_pairs={{0,96},{32,0},{64,32},{96,64},{1,97},{33,1},{65,33},{97,65},{2,98}... | collective-permute-start | bytes 811016 | tf_op jit(solution)/shard_map/ppermute | solution.py:444
  133.9 10.7 %collective-permute-start.12 = (bf16[96,1408]{1,0:T(8,128)(2,1)S(1)}, bf16[96,1408]{1,0:T(8,128)(2,1)S(1)}, u32[]{:S(2)}, u32[]{:S(2)}) collective-permute-start(bf16[96,1408]{1,0:T(8,128)(2,1)S(1)} %get-tuple-element.28), channel_id=1, source_target_pairs={{0,32},{32,64},{64,96},{96,0},{1,33},{33,65},{65,97},{97,1},{2,34}... | collective-permute-start | bytes 811016 | tf_op jit(solution)/shard_map/ppermute | solution.py:444
  138.7 10.2 %copy-start.2 = (bf16[1024,1024]{1,0:T(8,128)(2,1)S(1)}, bf16[1024,1024]{1,0:T(8,128)(2,1)}, u32[]{:S(2)}) copy-start(bf16[1024,1024]{1,0:T(8,128)(2,1)} %w_out_ref.1) | copy-start | bytes 6291460
  138.8 10.2 %collective-permute-start.14 = (bf16[96,1408]{1,0:T(8,128)(2,1)S(1)}, bf16[96,1408]{1,0:T(8,128)(2,1)S(1)}, u32[]{:S(2)}, u32[]{:S(2)}) collective-permute-start(bf16[96,1408]{1,0:T(8,128)(2,1)S(1)} %attend.4), channel_id=1, source_target_pairs={{0,64},{32,96},{64,0},{96,32},{1,65},{33,97},{65,1},{97,33},{2,66}... | collective-permute-start | bytes 811016 | tf_op jit(solution)/shard_map/ppermute | solution.py:444
